TPU v7x, 512 devices: a whole 4x4x16 slice. The times are simulated.
512 devices in a mesh: group: 16 (over y, x), dev: 32 (over z, core).
Axes of the slice: x: 4, y: 4, z: 16, core: 2. Of those that a mesh axis runs over, the one named last changes fastest.
Arguments:
- embeddings: float32 [262144, 768], P(('group', 'dev'))
- owner: int32 [262144], P(('group', 'dev')), may hold values from 0 to 31, as said below
Outputs:
- self_max: float32 [262144], P(('group', 'dev'))
- next_max: float32 [262144], P(('group', 'dev'))
- prev_max: float32 [262144], P(('group', 'dev'))
Inputs may be any that keep to these rules, and one draw needn't show every extreme that they name: `owner`: no device sends more than 32 of its vectors to one cluster; in each group one cluster takes exactly 32 vectors from every device of the group.
All inputs are finite; a program needn't handle non-finite values.
Results may differ from a plain program's by a relative error of at most 0.0004.
Values may be sent and summed in bfloat16 or wider, within the bound.
A program may use at most 64 MiB of HBM per device.

v0:
```python
import jax
import jax.numpy as jnp
from jax import lax
from jax.sharding import PartitionSpec as P


def extended(array, sides, width):
    for axis, dim in sides:
        size, length = (lax.axis_size(axis), array.shape[dim])
        up = [(i, (i + 1) % size) for i in range(size)]
        down = [(j, i) for i, j in up]
        last = lax.slice_in_dim(array, length - width, length, axis=dim)
        first = lax.slice_in_dim(array, 0, width, axis=dim)
        before = lax.ppermute(last, axis, up)
        after = lax.ppermute(first, axis, down)
        array = jnp.concatenate([before, array, after], axis=dim)
    return array


def side_by_side(arrays, axis, split_dim, concat_dim, along):
    both = jnp.concatenate(arrays, axis=along)
    out, at, done = (
        lax.all_to_all(both, axis, split_axis=split_dim, concat_axis=concat_dim, tiled=True),
        0,
        [],
    )
    for a in arrays:
        done.append(lax.slice_in_dim(out, at, at + a.shape[along], axis=along))
        at += a.shape[along]
    return tuple(done)


def unit_rows(embeddings):
    norm = jnp.sum(embeddings * embeddings, axis=-1, keepdims=True)
    return (embeddings * lax.rsqrt(norm + 1e-06)).astype(jnp.bfloat16)


def slot_ranks(owner_rows, owners):
    onehot = (owner_rows[:, None] == jnp.arange(owners, dtype=jnp.int32)[None, :]).astype(jnp.int32)
    before = jnp.cumsum(onehot, axis=0) - onehot
    return jnp.sum(before * onehot, axis=1)


def live_rows(slots):
    return jnp.einsum("sd,sd->s", slots, slots, preferred_element_type=jnp.float32) > 0.5


def best_match(left, right, live_right, skip_self):
    scores = jnp.dot(left, right.T, preferred_element_type=jnp.float32)
    keep = live_right[None, :]
    if skip_self:
        size = left.shape[0]
        same = lax.broadcasted_iota(jnp.int32, (size, size), 0) == lax.broadcasted_iota(
            jnp.int32, (size, size), 1
        )
        keep = keep & jnp.logical_not(same)
    return jnp.max(jnp.where(keep, scores, -1.0), axis=1)


def local(embeddings, owner):
    owners = lax.axis_size("dev")
    rows = embeddings.shape[0]
    width = embeddings.shape[1]
    capacity = max(2, 2 * rows // owners)
    unit = unit_rows(embeddings)
    ranks = slot_ranks(owner, owners)
    outgoing = jnp.zeros((owners, capacity, width), jnp.bfloat16).at[owner, ranks].set(unit)
    arrived = lax.all_to_all(outgoing, "dev", split_axis=0, concat_axis=0, tiled=True)
    slots = arrived.reshape(owners * capacity, width)
    total = slots.shape[0]
    live = live_rows(slots)
    self_slot = best_match(slots, slots, live, True)
    beside_all = extended(slots, (("group", 0),), total)
    before_slots = beside_all[:total]
    after_slots = beside_all[2 * total :]
    next_slot = best_match(slots, after_slots, live_rows(after_slots), False)
    prev_slot = best_match(slots, before_slots, live_rows(before_slots), False)
    shaped = (owners, capacity)
    back_self, back_next, back_prev = side_by_side(
        (self_slot.reshape(shaped), next_slot.reshape(shaped), prev_slot.reshape(shaped)),
        "dev",
        0,
        0,
        1,
    )
    return (back_self[owner, ranks], back_next[owner, ranks], back_prev[owner, ranks])


def solution(mesh):
    placed = (P(("group", "dev"), None), P(("group", "dev")))
    return jax.shard_map(
        local,
        mesh=mesh,
        in_specs=placed,
        out_specs=(P(("group", "dev")), P(("group", "dev")), P(("group", "dev"))),
        check_vma=False,
    )
```

profile of v0, /device:TPU:1, one launch (start us, length us, event | category | flops | bytes accessed | tf_op | source)
XLA Modules:
  0.0 211.6 jit_solution(14197398116018406094)
XLA Ops:
  0.6 0.0 copy-start
  0.6 0.0 copy-start.1
  0.6 1.7 multiply_reduce_fusion
  2.4 0.0 copy-done.1
  2.4 1.2 reduce-window.6
  3.6 0.2 slice_reduce_fusion
  3.8 0.1 fusion.7
  3.9 0.0 copy-done
  4.0 0.1 multiply_convert_fusion
  4.1 0.2 broadcast_in_dim.24
  4.3 29.9 %scatter_fusion = bf16[32,32,768]{2,1,0:T(8,128)(2,1)S(1)} fusion(bf16[32,32,768]{2,1,0:T(8,128)(2,1)S(1)} %broadcast_in_dim.24, s32[512]{0:T(512)S(1)} %bitcast.38, bf16[512,768]{1,0:T(8,128)(2,1)S(1)} %multiply_convert_fusion), kind=kCustom, calls=%fused_computation.3 | custom fusion | bytes 2363392 | tf_op jit(solution)/shard_map/scatter | solution.py:67
  34.3 95.1 %all_to_all.17 = bf16[32,32,768]{2,1,0:T(8,128)(2,1)S(1)} all-to-all(bf16[32,32,768]{2,1,0:T(8,128)(2,1)S(1)} %scatter_fusion), channel_id=1, replica_groups=mesh['group'=16,'dev'=32] {'dev'}, dimensions={0} | all-to-all | bytes 3145728 | tf_op jit(solution)/shard_map/all_to_all | solution.py:68
  129.4 3.1 %collective-permute-start.1 = (bf16[1024,768]{1,0:T(8,128)(2,1)S(1)}, bf16[1024,768]{1,0:T(8,128)(2,1)}, u32[]{:S(2)}, u32[]{:S(2)}) collective-permute-start(bf16[1024,768]{1,0:T(8,128)(2,1)S(1)} %bitcast.39), channel_id=1, source_target_pairs={{0,32},{32,64},{64,96},{96,128},{128,160},{160,192},{192,224},{224... | collective-permute-start | bytes 4718600 | tf_op jit(solution)/shard_map/ppermute | solution.py:14
  132.5 5.7 %collective-permute-start = (bf16[1024,768]{1,0:T(8,128)(2,1)S(1)}, bf16[1024,768]{1,0:T(8,128)(2,1)S(1)}, u32[]{:S(2)}, u32[]{:S(2)}) collective-permute-start(bf16[1024,768]{1,0:T(8,128)(2,1)S(1)} %bitcast.40), channel_id=1, source_target_pairs={{32,0},{64,32},{96,64},{128,96},{160,128},{192,160},{224,192},{256... | collective-permute-start | bytes 4718600 | tf_op jit(solution)/shard_map/ppermute | solution.py:15
  138.1 0.4 fusion.4
  138.6 1.8 select_reduce_fusion.2
  140.4 0.1 reshape.60
  140.5 30.0 %collective-permute-done.1 = bf16[1024,768]{1,0:T(8,128)(2,1)} collective-permute-done((bf16[1024,768]{1,0:T(8,128)(2,1)S(1)}, bf16[1024,768]{1,0:T(8,128)(2,1)}, u32[]{:S(2)}, u32[]{:S(2)}) %collective-permute-start.1) | collective-permute-done | bytes 1572896 | tf_op jit(solution)/shard_map/ppermute | solution.py:14
  170.5 1.8 fusion.2
  172.3 3.2 %select_reduce_fusion = f32[1024]{0:T(1024)S(1)} fusion(pred[1024]{0:T(1024)(128)(4,1)S(1)} %broadcast_compare_fusion, bf16[1024,768]{1,0:T(8,128)(2,1)S(1)} %bitcast.42, bf16[1024,768]{1,0:T(8,128)(2,1)} %collective-permute-done.1), kind=kOutput, calls=%fused_computation.4 | convolution fusion | flops 1612708864 | bytes 3150848 | tf_op jit(solution)/shard_map/dot_general | solution.py:49
  175.5 0.1 reshape.62
  175.6 0.0 collective-permute-done
  175.6 0.4 fusion.3
  176.0 1.8 select_reduce_fusion.1
  177.8 0.1 reshape.61
  177.9 0.1 pad_maximum_fusion
  178.0 15.7 %all_to_all.18 = f32[32,1,96]{2,1,0:T(1,128)S(1)} all-to-all(f32[32,1,96]{2,1,0:T(1,128)S(1)} %bitcast.45), channel_id=1, replica_groups=mesh['group'=16,'dev'=32] {'dev'}, dimensions={0} | all-to-all | bytes 24576 | tf_op jit(solution)/shard_map/all_to_all | solution.py:23
  193.7 0.1 fusion.11
  193.7 6.0 %gather_fusion.2 = f32[512]{0:T(512)} fusion(f32[32,32]{1,0:T(8,128)S(1)} %get-tuple-element.5, s32[512]{0:T(512)S(1)} %bitcast.35), kind=kCustom, calls=%fused_computation.2 | custom fusion | bytes 8192 | tf_op jit(solution)/shard_map/gather | solution.py:86
  199.7 6.0 %gather_fusion.1 = f32[512]{0:T(512)} fusion(f32[32,32]{1,0:T(8,128)S(1)} %get-tuple-element.6, s32[512]{0:T(512)S(1)} %bitcast.36), kind=kCustom, calls=%fused_computation.1 | custom fusion | bytes 8192 | tf_op jit(solution)/shard_map/gather | solution.py:86
  205.7 6.0 %gather_fusion = f32[512]{0:T(512)} fusion(f32[32,32]{1,0:T(8,128)S(1)} %get-tuple-element.7, s32[512]{0:T(512)S(1)} %bitcast.37), kind=kCustom, calls=%fused_computation | custom fusion | bytes 8192 | tf_op jit(solution)/shard_map/gather | solution.py:86
  (9 shorter events, 0.1 us)
Async XLA Ops:
  0.6 3.3 %copy-start = (f32[512,768]{1,0:T(8,128)S(1)}, f32[512,768]{1,0:T(8,128)}, u32[]{:S(2)}) copy-start(f32[512,768]{1,0:T(8,128)} %param.2) | copy-start | bytes 4718596
  0.6 1.7 copy-start.1
  129.4 41.1 %collective-permute-start.1 = (bf16[1024,768]{1,0:T(8,128)(2,1)S(1)}, bf16[1024,768]{1,0:T(8,128)(2,1)}, u32[]{:S(2)}, u32[]{:S(2)}) collective-permute-start(bf16[1024,768]{1,0:T(8,128)(2,1)S(1)} %bitcast.39), channel_id=1, source_target_pairs={{0,32},{32,64},{64,96},{96,128},{128,160},{160,192},{192,224},{224... | collective-permute-start | bytes 4718600 | tf_op jit(solution)/shard_map/ppermute | solution.py:14
  132.5 43.2 %collective-permute-start = (bf16[1024,768]{1,0:T(8,128)(2,1)S(1)}, bf16[1024,768]{1,0:T(8,128)(2,1)S(1)}, u32[]{:S(2)}, u32[]{:S(2)}) collective-permute-start(bf16[1024,768]{1,0:T(8,128)(2,1)S(1)} %bitcast.40), channel_id=1, source_target_pairs={{32,0},{64,32},{96,64},{128,96},{160,128},{192,160},{224,192},{256... | collective-permute-start | bytes 4718600 | tf_op jit(solution)/shard_map/ppermute | solution.py:15
where the time goes:
time: 212 us
  blocking collectives  111 us (52%)
  local copies, waits for them, and re-layouts  48.5 us (23%)
  waiting for transfers between devices  30 us (14%)
  starting transfers between devices  8.76 us (4%)
  matrix products  6.91 us (3%)
  other arithmetic  5.86 us (3%)
    all_to_all x1, blocking collectives, local(): lax.all_to_all(outgoing, 'dev', split_axis=0, concat_axis=0, tiled=True)  95.1 us
    ppermute x1, waiting for transfers between devices, extended(): before = lax.ppermute(last, axis, up)  30 us
    scatter x1, local copies, waits for them, and re-layouts, local(): jnp.zeros((owners, capacity, width), jnp.bfloat16).at[owner, ranks]  29.9 us
    all_to_all x1, blocking collectives, side_by_side(): lax.all_to_all(both, axis, split_axis=split_dim, concat_axis=concat_dim,...  15.7 us
    dot_general x3, matrix products, best_match(): scores = jnp.dot(left, right.T, preferred_element_type=jnp.float32)  6.91 us
    gather x1, local copies, waits for them, and re-layouts, local(): back_prev[owner, ranks]  5.97 us
    gather x1, local copies, waits for them, and re-layouts, local(): back_next[owner, ranks]  5.96 us
    gather x1, local copies, waits for them, and re-layouts, local(): back_self[owner, ranks]  5.96 us
  transfers between devices with their start and end apart: 2, of which 1 were waited for; matrix products, arithmetic and copies ran while one was open for 4% of the time, Pallas kernels for 0%

commit v1 on v0

v1 whole, which is shorter than its diff:
```python
import functools

import jax
import jax.numpy as jnp
from jax import lax
from jax.experimental import pallas as pl
from jax.experimental.pallas import tpu as pltpu
from jax.sharding import PartitionSpec as P

CAP = 32
DEAD = 2.0
STAGE = 8
PIECE = 4
MESH = pl.DeviceIdType.MESH


def ring_offset(k, nz):
    j = k // 2
    size = nz // 2 - (j + 1) // 2
    return jnp.where(j % 2 == 1, size, -size)


def kernel(
    emb_hbm,
    owner_ref,
    self_ref,
    next_ref,
    prev_ref,
    emb,
    unit,
    outgoing,
    own,
    before,
    after,
    acc,
    ret,
    got,
    load_sem,
    send_sem,
    recv_sem,
    pair_send,
    pair_recv,
    ret_send,
    ret_recv,
    *,
    groups,
    owners,
):
    rows, width = emb.shape
    nz = owners // 2
    group = lax.axis_index("group")
    me = lax.axis_index("dev")
    mez, mec = me // 2, me % 2
    stages = owners // STAGE
    here = owners - 2

    load = pltpu.make_async_copy(emb_hbm, emb, load_sem)
    load.start()

    def target(k):
        z = (mez + ring_offset(k, nz) + nz) % nz
        return 2 * z + (mec + k) % 2

    def source(k):
        z = (mez - ring_offset(k, nz) + nz) % nz
        return 2 * z + (mec + k) % 2

    barrier = pltpu.get_barrier_semaphore()

    def greet(d, carry):
        pl.semaphore_signal(barrier, inc=1, device_id={"dev": (me + d) % owners}, device_id_type=MESH)
        return carry

    lax.fori_loop(1, owners, greet, 0)
    later = (group + 1) % groups
    earlier = (group + groups - 1) % groups
    pl.semaphore_signal(barrier, inc=1, device_id={"group": later}, device_id_type=MESH)
    pl.semaphore_signal(barrier, inc=1, device_id={"group": earlier}, device_id_type=MESH)

    owner = jnp.concatenate([owner_ref[a : a + 1, :] for a in range(rows // 128)], axis=1)
    chunk = lax.broadcasted_iota(jnp.int32, (owners, 1), 0)
    cluster = 2 * ((mez + ring_offset(chunk, nz) + nz) % nz) + (mec + chunk) % 2
    hot = owner == cluster
    hot_f = jnp.where(hot, 1.0, 0.0)
    hot_b = hot_f.astype(jnp.bfloat16)
    earlier_row = lax.broadcasted_iota(jnp.int32, (rows, rows), 0) < lax.broadcasted_iota(
        jnp.int32, (rows, rows), 1
    )
    ahead = jnp.dot(
        hot_b, jnp.where(earlier_row, 1.0, 0.0).astype(jnp.bfloat16), preferred_element_type=jnp.float32
    )
    rank = jnp.sum(ahead * hot_f, axis=0, keepdims=True).astype(jnp.int32)
    chunk_of = jnp.sum(hot_f * chunk.astype(jnp.float32), axis=0, keepdims=True).astype(jnp.int32)
    slot_of = chunk_of * CAP + rank
    count = jnp.sum(hot_f, axis=1, keepdims=True)

    load.wait()
    raw = emb[...]
    norm = jnp.sum(raw * raw, axis=-1, keepdims=True)
    unit[...] = (raw * lax.rsqrt(norm + 1e-06)).astype(jnp.bfloat16)

    def dispatch(k):
        return pltpu.make_async_remote_copy(
            src_ref=outgoing.at[k],
            dst_ref=own.at[k],
            send_sem=send_sem.at[k],
            recv_sem=recv_sem.at[k],
            device_id={"dev": target(k)},
            device_id_type=MESH,
        )

    def start_dispatch(k, carry):
        dispatch(k).start()
        return carry

    slot = lax.broadcasted_iota(jnp.int32, (STAGE * CAP, 1), 0)
    first = lax.broadcasted_iota(jnp.int32, (CAP, width), 1) == 0
    in_chunk = lax.broadcasted_iota(jnp.int32, (CAP, width), 0).astype(jnp.float32)
    for t in range(stages):
        pick = jnp.where(slot_of == slot + t * STAGE * CAP, 1.0, 0.0).astype(jnp.bfloat16)
        packed = jnp.dot(pick, unit[...], preferred_element_type=jnp.float32)
        for c in range(STAGE):
            k = t * STAGE + c
            empty = first & (in_chunk >= count[k : k + 1, :])
            piece = jnp.where(empty, DEAD, packed[c * CAP : (c + 1) * CAP, :]).astype(jnp.bfloat16)
            if k == here:
                own[k] = piece
            else:
                outgoing[k] = piece
        if t == 0:
            pl.semaphore_wait(barrier, owners + 1)
        if t < stages - 1:
            lax.fori_loop(t * STAGE, (t + 1) * STAGE, start_dispatch, 0)
        else:
            lax.fori_loop(t * STAGE, here, start_dispatch, 0)
            dispatch(owners - 1).start()

    acc[...] = jnp.full_like(acc, -4.0)

    def forward(p, way):
        part = pl.ds(p * PIECE, PIECE)
        return pltpu.make_async_remote_copy(
            src_ref=own.at[part],
            dst_ref=(before if way == 0 else after).at[part],
            send_sem=pair_send.at[way, p],
            recv_sem=pair_recv.at[way, p],
            device_id={"group": later if way == 0 else earlier},
            device_id_type=MESH,
        )

    def block(which, found, jb, ib, diagonal=False):
        right = found[pl.ds(jb * STAGE, STAGE)].reshape(STAGE * CAP, width)
        left = own[pl.ds(ib * STAGE, STAGE)].reshape(STAGE * CAP, width)
        scores = lax.dot_general(right, left, (((1,), (1,)), ((), ())), preferred_element_type=jnp.float32)
        drop = right[:, :128].astype(jnp.float32)[:, 0:1] > 1.5
        if diagonal:
            size = STAGE * CAP
            drop = drop | (
                lax.broadcasted_iota(jnp.int32, (size, size), 0) == lax.broadcasted_iota(jnp.int32, (size, size), 1)
            )
        scores = jnp.where(drop, -1.0, scores)
        best = jnp.max(scores.reshape(STAGE * CAP // 8, 8, STAGE * CAP), axis=0)
        acc[which, ib] = jnp.maximum(acc[which, ib], best)

    def arrive(t):
        def chunk_arrives(k, carry):
            dispatch(k).wait_recv()
            return carry

        def piece_arrives(p, carry):
            lax.fori_loop(p * PIECE, (p + 1) * PIECE, chunk_arrives, 0)
            forward(p, 0).start()
            forward(p, 1).start()
            return carry

        per = STAGE // PIECE
        if t < stages - 1:
            lax.fori_loop(t * per, (t + 1) * per, piece_arrives, 0)
        else:
            lax.fori_loop(t * per, (t + 1) * per - 1, piece_arrives, 0)
            lax.fori_loop(owners - PIECE, here, chunk_arrives, 0)
            dispatch(owners - 1).wait_recv()
            forward((t + 1) * per - 1, 0).start()
            forward((t + 1) * per - 1, 1).start()

    def pair_arrives(t):
        def piece(p, carry):
            forward(p, 0).wait_recv()
            forward(p, 1).wait_recv()
            return carry

        per = STAGE // PIECE
        lax.fori_loop(t * per, (t + 1) * per, piece, 0)

    def both(jb, ib):
        block(1, after, jb, ib)
        block(2, before, jb, ib)

    for t in range(stages):
        arrive(t)
        block(0, own, t, t, diagonal=True)

        def own_blocks(b, carry, t=t):
            block(0, own, t, b)
            block(0, own, b, t)
            return carry

        lax.fori_loop(0, t, own_blocks, 0)
        if t > 0:
            pair_arrives(t - 1)

            def new_rows(b, carry, t=t):
                both(b, t)
                return carry

            def new_found(b, carry, t=t):
                both(t - 1, b)
                return carry

            lax.fori_loop(0, t, new_rows, 0)
            lax.fori_loop(0, t, new_found, 0)
    pair_arrives(stages - 1)

    def last_found(b, carry):
        both(stages - 1, b)
        return carry

    lax.fori_loop(0, stages, last_found, 0)

    tiles = []
    for which in range(3):
        parts = []
        for b in range(stages):
            best = jnp.max(acc[which, b], axis=0, keepdims=True)
            parts += [best[:, h * 128 : (h + 1) * 128] for h in range(STAGE * CAP // 128)]
        tiles.append(jnp.concatenate(parts, axis=0))
    lane = lax.broadcasted_iota(jnp.int32, tiles[0].shape, 1)
    per_tile = 128 // CAP
    for j in range(per_tile):
        moved = [pltpu.roll(tiles[w], (CAP * (w - j)) % 128, 1) if (w - j) % 4 else tiles[w] for w in range(3)]
        mixed = jnp.where(lane < CAP, moved[0], jnp.where(lane < 2 * CAP, moved[1], moved[2]))
        for t in range(owners // per_tile):
            k = per_tile * t + j
            if k == here:
                got[k] = mixed[t : t + 1, :]
            else:
                ret[k] = mixed[t : t + 1, :]

    def give_back(k):
        return pltpu.make_async_remote_copy(
            src_ref=ret.at[k],
            dst_ref=got.at[k],
            send_sem=ret_send.at[k],
            recv_sem=ret_recv.at[k],
            device_id={"dev": source(k)},
            device_id_type=MESH,
        )

    def start_back(k, carry):
        give_back(k).start()
        return carry

    lax.fori_loop(0, here, start_back, 0)
    give_back(owners - 1).start()

    def drain(k, carry):
        dispatch(k).wait_send()
        return carry

    lax.fori_loop(0, here, drain, 0)
    dispatch(owners - 1).wait_send()

    def drain_pair(p, carry):
        forward(p, 0).wait_send()
        forward(p, 1).wait_send()
        return carry

    lax.fori_loop(0, owners // PIECE, drain_pair, 0)

    def wait_back(k, carry):
        give_back(k).wait()
        return carry

    lax.fori_loop(0, here, wait_back, 0)
    give_back(owners - 1).wait()

    table = got[...].reshape(owners, 128)
    high = table.astype(jnp.bfloat16)
    rest = table - high.astype(jnp.float32)
    middle = rest.astype(jnp.bfloat16)
    low = (rest - middle.astype(jnp.float32)).astype(jnp.bfloat16)
    stacked = jnp.concatenate([high, middle, low], axis=0)
    picks = jnp.concatenate([hot_b, hot_b, hot_b], axis=0)
    found = lax.dot_general(stacked, picks, (((0,), (0,)), ((), ())), preferred_element_type=jnp.float32)
    mine = lax.broadcasted_iota(jnp.int32, (CAP, 1), 0) == rank
    for which, ref in enumerate((self_ref, next_ref, prev_ref)):
        kept = jnp.where(mine, found[which * CAP : (which + 1) * CAP, :], 0.0)
        line = jnp.sum(kept, axis=0, keepdims=True)
        for a in range(rows // 128):
            ref[a : a + 1, :] = line[:, a * 128 : (a + 1) * 128]


def local(embeddings, owner):
    owners = lax.axis_size("dev")
    groups = lax.axis_size("group")
    rows, width = embeddings.shape
    vmem = pl.BlockSpec(memory_space=pltpu.VMEM)
    slots = (owners, CAP, width)
    result = jax.ShapeDtypeStruct((rows // 128, 128), jnp.float32)
    outs = pl.pallas_call(
        functools.partial(kernel, groups=groups, owners=owners),
        out_shape=(result, result, result),
        in_specs=[pl.BlockSpec(memory_space=pl.ANY), vmem],
        out_specs=(vmem, vmem, vmem),
        scratch_shapes=[
            pltpu.VMEM((rows, width), jnp.float32),
            pltpu.VMEM((rows, width), jnp.bfloat16),
            pltpu.VMEM(slots, jnp.bfloat16),
            pltpu.VMEM(slots, jnp.bfloat16),
            pltpu.VMEM(slots, jnp.bfloat16),
            pltpu.VMEM(slots, jnp.bfloat16),
            pltpu.VMEM((3, owners // STAGE, 8, STAGE * CAP), jnp.float32),
            pltpu.VMEM((owners, 1, 128), jnp.float32),
            pltpu.VMEM((owners, 1, 128), jnp.float32),
            pltpu.SemaphoreType.DMA,
            pltpu.SemaphoreType.DMA((owners,)),
            pltpu.SemaphoreType.DMA((owners,)),
            pltpu.SemaphoreType.DMA((2, owners // PIECE)),
            pltpu.SemaphoreType.DMA((2, owners // PIECE)),
            pltpu.SemaphoreType.DMA((owners,)),
            pltpu.SemaphoreType.DMA((owners,)),
        ],
        compiler_params=pltpu.CompilerParams(
            collective_id=0, has_side_effects=True, vmem_limit_bytes=40 * 1024 * 1024
        ),
    )(embeddings, owner.reshape(rows // 128, 128))
    return tuple(o.reshape(rows) for o in outs)


def solution(mesh):
    placed = (P(("group", "dev"), None), P(("group", "dev")))
    return jax.shard_map(
        local,
        mesh=mesh,
        in_specs=placed,
        out_specs=(P(("group", "dev")), P(("group", "dev")), P(("group", "dev"))),
        check_vma=False,
    )
```

time: 212 us -> 118 us (0.56)
  Pallas kernels: 0 us -> 113 us
  blocking collectives: 111 us -> 0 us
  local copies, waits for them, and re-layouts: 48.5 us -> 3.82 us
  waiting for transfers between devices: 30 us -> 0 us
  starting transfers between devices: 8.76 us -> 0 us
  matrix products: 6.91 us -> 0 us
  other arithmetic: 5.86 us -> 0 us
    pallas_call x0 -> x1, Pallas kernels: none -> 113 us  [local(): pl.pallas_call(functools.partial(kernel, groups=groups, owners=owners), o...]
    all_to_all x2 -> x0, blocking collectives: 111 us -> none  [the longest x1 95.1 us: local(): lax.all_to_all(outgoing, 'dev', split_axis=0, concat_axis=0, tiled=True)]
    ppermute x2 -> x0, waiting for transfers between devices: 30 us -> none  [the longest x1 30 us: extended(): before = lax.ppermute(last, axis, up)]
    scatter x1 -> x0, local copies, waits for them, and re-layouts: 29.9 us -> none  [local(): jnp.zeros((owners, capacity, width), jnp.bfloat16).at[owner, ranks]]
    gather x3 -> x0, local copies, waits for them, and re-layouts: 17.9 us -> none  [the longest x1 5.97 us: local(): back_prev[owner, ranks]]
    ppermute x2 -> x0, starting transfers between devices: 8.76 us -> none  [the longest x1 5.68 us: extended(): after = lax.ppermute(first, axis, down)]
    dot_general x3 -> x0, matrix products: 6.91 us -> none  [best_match(): scores = jnp.dot(left, right.T, preferred_element_type=jnp.float32)]
    unnamed x4 -> x7, local copies, waits for them, and re-layouts: 0.01 us -> 3.82 us
  transfers between devices with their start and end apart: 2 -> 0, of which waited for: 1 -> 0; matrix products, arithmetic and copies ran while one was open for 4% -> 0% of each run, Pallas kernels for 0% -> 0%
where the time goes in v1:
time: 118 us
  Pallas kernels  113 us (96%)
  local copies, waits for them, and re-layouts  3.82 us (3%)
    pallas_call x1, Pallas kernels, local(): pl.pallas_call(functools.partial(kernel, groups=groups, owners=owners), o...  113 us
    unnamed x7, local copies, waits for them, and re-layouts  3.82 us

profile of v1, /device:TPU:1, one launch (start us, length us, event | category | flops | bytes accessed | tf_op | source)
XLA Modules:
  0.0 117.7 jit_solution(15351850053076544744)
XLA Ops:
  0.6 0.0 copy-start
  0.6 1.4 %copy-done = f32[512,768]{1,0:T(8,128)S(1)} copy-done((f32[512,768]{1,0:T(8,128)S(1)}, f32[512,768]{1,0:T(8,128)}, u32[]{:S(2)}) %copy-start) | copy-done | bytes 1572888
  2.0 0.0 copy-start.1
  2.0 0.7 copy-done.1
  2.7 113.2 %shard_map.49 = (f32[4,128]{1,0:T(4,128)S(1)}, f32[4,128]{1,0:T(4,128)S(1)}, f32[4,128]{1,0:T(4,128)S(1)}) custom-call(f32[512,768]{1,0:T(8,128)S(1)} %copy-done, s32[4,128]{1,0:T(4,128)S(1)} %bitcast.4), custom_call_target="tpu_custom_call" | custom-call | tf_op jit(solution)/shard_map/pallas_call | solution.py:310
  115.9 0.6 copy.8
  116.5 0.6 copy.9
  117.1 0.6 copy.10
Async XLA Ops:
  0.6 1.4 %copy-start = (f32[512,768]{1,0:T(8,128)S(1)}, f32[512,768]{1,0:T(8,128)}, u32[]{:S(2)}) copy-start(f32[512,768]{1,0:T(8,128)} %emb_hbm.1) | copy-start | bytes 4718596
  2.0 0.7 copy-start.1

commit v2 on v1

--- a/solution.py
+++ b/solution.py
@@ -10,23 +10,24 @@
 CAP = 32
 DEAD = 2.0
 STAGE = 8
-PIECE = 4
+PIECE = 1
+PACK = 4
+RELAYED = (2, 3)
 MESH = pl.DeviceIdType.MESH
 
 
 def ring_offset(k, nz):
     j = k // 2
-    size = nz // 2 - (j + 1) // 2
-    return jnp.where(j % 2 == 1, size, -size)
+    size = jnp.where(j == 0, 0, nz // 2 - j // 2)
+    return jnp.where(j % 2 == 0, size, -size)
 
 
 def kernel(
     emb_hbm,
+    owner_hbm,
+    out_ref,
+    emb,
     owner_ref,
-    self_ref,
-    next_ref,
-    prev_ref,
-    emb,
     unit,
     outgoing,
     own,
@@ -35,6 +36,7 @@
     acc,
     ret,
     got,
+    relay,
     load_sem,
     send_sem,
     recv_sem,
@@ -42,6 +44,8 @@
     pair_recv,
     ret_send,
     ret_recv,
+    relay_send,
+    relay_recv,
     *,
     groups,
     owners,
@@ -52,9 +56,11 @@
     me = lax.axis_index("dev")
     mez, mec = me // 2, me % 2
     stages = owners // STAGE
-    here = owners - 2
-
-    load = pltpu.make_async_copy(emb_hbm, emb, load_sem)
+    here = 0
+
+    load_owner = pltpu.make_async_copy(owner_hbm, owner_ref, load_sem.at[0])
+    load_owner.start()
+    load = pltpu.make_async_copy(emb_hbm, emb, load_sem.at[1])
     load.start()
 
     def target(k):
@@ -76,6 +82,8 @@
     earlier = (group + groups - 1) % groups
     pl.semaphore_signal(barrier, inc=1, device_id={"group": later}, device_id_type=MESH)
     pl.semaphore_signal(barrier, inc=1, device_id={"group": earlier}, device_id_type=MESH)
+
+    load_owner.wait()
 
     owner = jnp.concatenate([owner_ref[a : a + 1, :] for a in range(rows // 128)], axis=1)
     chunk = lax.broadcasted_iota(jnp.int32, (owners, 1), 0)
@@ -113,14 +121,36 @@
         dispatch(k).start()
         return carry
 
-    slot = lax.broadcasted_iota(jnp.int32, (STAGE * CAP, 1), 0)
+    def to_relay(i):
+        z = (mez + (1, nz - 1)[i]) % nz
+        return pltpu.make_async_remote_copy(
+            src_ref=outgoing.at[RELAYED[i]],
+            dst_ref=relay.at[i],
+            send_sem=send_sem.at[RELAYED[i]],
+            recv_sem=relay_recv.at[i],
+            device_id={"dev": 2 * z + mec},
+            device_id_type=MESH,
+        )
+
+    def from_relay(i):
+        z = (mez + (nz // 2 - 1, nz // 2 + 1)[i]) % nz
+        return pltpu.make_async_remote_copy(
+            src_ref=relay.at[i],
+            dst_ref=own.at[RELAYED[i]],
+            send_sem=relay_send.at[i],
+            recv_sem=recv_sem.at[RELAYED[i]],
+            device_id={"dev": 2 * z + (mec + RELAYED[i]) % 2},
+            device_id_type=MESH,
+        )
+
+    slot = lax.broadcasted_iota(jnp.int32, (PACK * CAP, 1), 0)
     first = lax.broadcasted_iota(jnp.int32, (CAP, width), 1) == 0
     in_chunk = lax.broadcasted_iota(jnp.int32, (CAP, width), 0).astype(jnp.float32)
-    for t in range(stages):
-        pick = jnp.where(slot_of == slot + t * STAGE * CAP, 1.0, 0.0).astype(jnp.bfloat16)
+    for t in range(owners // PACK):
+        pick = jnp.where(slot_of == slot + t * PACK * CAP, 1.0, 0.0).astype(jnp.bfloat16)
         packed = jnp.dot(pick, unit[...], preferred_element_type=jnp.float32)
-        for c in range(STAGE):
-            k = t * STAGE + c
+        for c in range(PACK):
+            k = t * PACK + c
             empty = first & (in_chunk >= count[k : k + 1, :])
             piece = jnp.where(empty, DEAD, packed[c * CAP : (c + 1) * CAP, :]).astype(jnp.bfloat16)
             if k == here:
@@ -129,11 +159,15 @@
                 outgoing[k] = piece
         if t == 0:
             pl.semaphore_wait(barrier, owners + 1)
-        if t < stages - 1:
-            lax.fori_loop(t * STAGE, (t + 1) * STAGE, start_dispatch, 0)
+            to_relay(0).start()
+            to_relay(1).start()
+            dispatch(1).start()
         else:
-            lax.fori_loop(t * STAGE, here, start_dispatch, 0)
-            dispatch(owners - 1).start()
+            lax.fori_loop(t * PACK, (t + 1) * PACK, start_dispatch, 0)
+        if t == owners // PACK // 2:
+            for i in range(2):
+                to_relay(i).wait_recv()
+                from_relay(i).start()
 
     acc[...] = jnp.full_like(acc, -4.0)
 
@@ -174,14 +208,13 @@
             return carry
 
         per = STAGE // PIECE
-        if t < stages - 1:
+        if t == 0:
+            lax.fori_loop(1, PIECE, chunk_arrives, 0)
+            forward(0, 0).start()
+            forward(0, 1).start()
+            lax.fori_loop(1, per, piece_arrives, 0)
+        else:
             lax.fori_loop(t * per, (t + 1) * per, piece_arrives, 0)
-        else:
-            lax.fori_loop(t * per, (t + 1) * per - 1, piece_arrives, 0)
-            lax.fori_loop(owners - PIECE, here, chunk_arrives, 0)
-            dispatch(owners - 1).wait_recv()
-            forward((t + 1) * per - 1, 0).start()
-            forward((t + 1) * per - 1, 1).start()
 
     def pair_arrives(t):
         def piece(p, carry):
@@ -260,15 +293,16 @@
         give_back(k).start()
         return carry
 
-    lax.fori_loop(0, here, start_back, 0)
-    give_back(owners - 1).start()
+    lax.fori_loop(2, owners, start_back, 0)
+    give_back(1).start()
 
     def drain(k, carry):
         dispatch(k).wait_send()
         return carry
 
-    lax.fori_loop(0, here, drain, 0)
-    dispatch(owners - 1).wait_send()
+    lax.fori_loop(1, owners, drain, 0)
+    for i in range(2):
+        from_relay(i).wait_send()
 
     def drain_pair(p, carry):
         forward(p, 0).wait_send()
@@ -281,8 +315,7 @@
         give_back(k).wait()
         return carry
 
-    lax.fori_loop(0, here, wait_back, 0)
-    give_back(owners - 1).wait()
+    lax.fori_loop(1, owners, wait_back, 0)
 
     table = got[...].reshape(owners, 128)
     high = table.astype(jnp.bfloat16)
@@ -293,11 +326,11 @@
     picks = jnp.concatenate([hot_b, hot_b, hot_b], axis=0)
     found = lax.dot_general(stacked, picks, (((0,), (0,)), ((), ())), preferred_element_type=jnp.float32)
     mine = lax.broadcasted_iota(jnp.int32, (CAP, 1), 0) == rank
-    for which, ref in enumerate((self_ref, next_ref, prev_ref)):
+    for which in range(3):
         kept = jnp.where(mine, found[which * CAP : (which + 1) * CAP, :], 0.0)
         line = jnp.sum(kept, axis=0, keepdims=True)
         for a in range(rows // 128):
-            ref[a : a + 1, :] = line[:, a * 128 : (a + 1) * 128]
+            out_ref[which, a : a + 1, :] = line[:, a * 128 : (a + 1) * 128]
 
 
 def local(embeddings, owner):
@@ -306,14 +339,15 @@
     rows, width = embeddings.shape
     vmem = pl.BlockSpec(memory_space=pltpu.VMEM)
     slots = (owners, CAP, width)
-    result = jax.ShapeDtypeStruct((rows // 128, 128), jnp.float32)
-    outs = pl.pallas_call(
+    hbm = pl.BlockSpec(memory_space=pltpu.HBM)
+    out = pl.pallas_call(
         functools.partial(kernel, groups=groups, owners=owners),
-        out_shape=(result, result, result),
-        in_specs=[pl.BlockSpec(memory_space=pl.ANY), vmem],
-        out_specs=(vmem, vmem, vmem),
+        out_shape=jax.ShapeDtypeStruct((3, rows // 128, 128), jnp.float32),
+        in_specs=[hbm, hbm],
+        out_specs=vmem,
         scratch_shapes=[
             pltpu.VMEM((rows, width), jnp.float32),
+            pltpu.VMEM((rows // 128, 128), jnp.int32),
             pltpu.VMEM((rows, width), jnp.bfloat16),
             pltpu.VMEM(slots, jnp.bfloat16),
             pltpu.VMEM(slots, jnp.bfloat16),
@@ -322,19 +356,22 @@
             pltpu.VMEM((3, owners // STAGE, 8, STAGE * CAP), jnp.float32),
             pltpu.VMEM((owners, 1, 128), jnp.float32),
             pltpu.VMEM((owners, 1, 128), jnp.float32),
-            pltpu.SemaphoreType.DMA,
+            pltpu.VMEM((2, CAP, width), jnp.bfloat16),
+            pltpu.SemaphoreType.DMA((2,)),
             pltpu.SemaphoreType.DMA((owners,)),
             pltpu.SemaphoreType.DMA((owners,)),
             pltpu.SemaphoreType.DMA((2, owners // PIECE)),
             pltpu.SemaphoreType.DMA((2, owners // PIECE)),
             pltpu.SemaphoreType.DMA((owners,)),
             pltpu.SemaphoreType.DMA((owners,)),
+            pltpu.SemaphoreType.DMA((2,)),
+            pltpu.SemaphoreType.DMA((2,)),
         ],
         compiler_params=pltpu.CompilerParams(
-            collective_id=0, has_side_effects=True, vmem_limit_bytes=40 * 1024 * 1024
+            collective_id=0, has_side_effects=True, vmem_limit_bytes=60 * 1024 * 1024
         ),
     )(embeddings, owner.reshape(rows // 128, 128))
-    return tuple(o.reshape(rows) for o in outs)
+    return tuple(out[which].reshape(rows) for which in range(3))
 
 
 def solution(mesh):

time: 118 us -> 127 us (1.076)
  Pallas kernels: 113 us -> 125 us
  local copies, waits for them, and re-layouts: 3.82 us -> 1.27 us
    pallas_call x1, Pallas kernels: 113 us -> 125 us  [local(): pl.pallas_call(functools.partial(kernel, groups=groups, owners=owners), o...]
    unnamed x7 -> x0, local copies, waits for them, and re-layouts: 3.82 us -> none
    another operation x0 -> x1, local copies, waits for them, and re-layouts: none -> 1.27 us  [local(): return tuple((out[which].reshape(rows) for which in range(3)))]
where the time goes in v2:
time: 127 us
  Pallas kernels  125 us (98%)
  local copies, waits for them, and re-layouts  1.27 us (1%)
    pallas_call x1, Pallas kernels, local(): pl.pallas_call(functools.partial(kernel, groups=groups, owners=owners), o...  125 us

profile of v2, /device:TPU:1, one launch (start us, length us, event | category | flops | bytes accessed | tf_op | source)
XLA Modules:
  0.0 127.0 jit_solution(6364853082527793852)
XLA Ops:
  0.6 125.1 %shard_map.49 = f32[3,4,128]{2,1,0:T(4,128)} custom-call(f32[512,768]{1,0:T(8,128)} %emb_hbm.1, s32[4,128]{1,0:T(4,128)} %bitcast.7), custom_call_target="tpu_custom_call" | custom-call | tf_op jit(solution)/shard_map/pallas_call | solution.py:343
  125.8 1.3 slice_bitcast_fusion

commit v3 on v2

--- a/solution.py
+++ b/solution.py
@@ -12,14 +12,13 @@
 STAGE = 8
 PIECE = 1
 PACK = 4
-RELAYED = (2, 3)
 MESH = pl.DeviceIdType.MESH
 
 
 def ring_offset(k, nz):
     j = k // 2
-    size = jnp.where(j == 0, 0, nz // 2 - j // 2)
-    return jnp.where(j % 2 == 0, size, -size)
+    size = (j + 1) // 2
+    return jnp.where(j % 2 == 1, size, -size)
 
 
 def kernel(
@@ -36,7 +35,6 @@
     acc,
     ret,
     got,
-    relay,
     load_sem,
     send_sem,
     recv_sem,
@@ -44,8 +42,6 @@
     pair_recv,
     ret_send,
     ret_recv,
-    relay_send,
-    relay_recv,
     *,
     groups,
     owners,
@@ -121,28 +117,6 @@
         dispatch(k).start()
         return carry
 
-    def to_relay(i):
-        z = (mez + (1, nz - 1)[i]) % nz
-        return pltpu.make_async_remote_copy(
-            src_ref=outgoing.at[RELAYED[i]],
-            dst_ref=relay.at[i],
-            send_sem=send_sem.at[RELAYED[i]],
-            recv_sem=relay_recv.at[i],
-            device_id={"dev": 2 * z + mec},
-            device_id_type=MESH,
-        )
-
-    def from_relay(i):
-        z = (mez + (nz // 2 - 1, nz // 2 + 1)[i]) % nz
-        return pltpu.make_async_remote_copy(
-            src_ref=relay.at[i],
-            dst_ref=own.at[RELAYED[i]],
-            send_sem=relay_send.at[i],
-            recv_sem=recv_sem.at[RELAYED[i]],
-            device_id={"dev": 2 * z + (mec + RELAYED[i]) % 2},
-            device_id_type=MESH,
-        )
-
     slot = lax.broadcasted_iota(jnp.int32, (PACK * CAP, 1), 0)
     first = lax.broadcasted_iota(jnp.int32, (CAP, width), 1) == 0
     in_chunk = lax.broadcasted_iota(jnp.int32, (CAP, width), 0).astype(jnp.float32)
@@ -159,15 +133,7 @@
                 outgoing[k] = piece
         if t == 0:
             pl.semaphore_wait(barrier, owners + 1)
-            to_relay(0).start()
-            to_relay(1).start()
-            dispatch(1).start()
-        else:
-            lax.fori_loop(t * PACK, (t + 1) * PACK, start_dispatch, 0)
-        if t == owners // PACK // 2:
-            for i in range(2):
-                to_relay(i).wait_recv()
-                from_relay(i).start()
+        lax.fori_loop(max(t * PACK, 1), (t + 1) * PACK, start_dispatch, 0)
 
     acc[...] = jnp.full_like(acc, -4.0)
 
@@ -293,16 +259,13 @@
         give_back(k).start()
         return carry
 
-    lax.fori_loop(2, owners, start_back, 0)
-    give_back(1).start()
+    lax.fori_loop(1, owners, start_back, 0)
 
     def drain(k, carry):
         dispatch(k).wait_send()
         return carry
 
     lax.fori_loop(1, owners, drain, 0)
-    for i in range(2):
-        from_relay(i).wait_send()
 
     def drain_pair(p, carry):
         forward(p, 0).wait_send()
@@ -356,7 +319,6 @@
             pltpu.VMEM((3, owners // STAGE, 8, STAGE * CAP), jnp.float32),
             pltpu.VMEM((owners, 1, 128), jnp.float32),
             pltpu.VMEM((owners, 1, 128), jnp.float32),
-            pltpu.VMEM((2, CAP, width), jnp.bfloat16),
             pltpu.SemaphoreType.DMA((2,)),
             pltpu.SemaphoreType.DMA((owners,)),
             pltpu.SemaphoreType.DMA((owners,)),
@@ -364,8 +326,6 @@
             pltpu.SemaphoreType.DMA((2, owners // PIECE)),
             pltpu.SemaphoreType.DMA((owners,)),
             pltpu.SemaphoreType.DMA((owners,)),
-            pltpu.SemaphoreType.DMA((2,)),
-            pltpu.SemaphoreType.DMA((2,)),
         ],
         compiler_params=pltpu.CompilerParams(
             collective_id=0, has_side_effects=True, vmem_limit_bytes=60 * 1024 * 1024

time: 127 us -> 111 us (0.87)
  Pallas kernels: 125 us -> 109 us
    pallas_call x1, Pallas kernels: 125 us -> 109 us  [local(): pl.pallas_call(functools.partial(kernel, groups=groups, owners=owners), o...]
where the time goes in v3:
time: 111 us
  Pallas kernels  109 us (98%)
  local copies, waits for them, and re-layouts  1.27 us (1%)
    pallas_call x1, Pallas kernels, local(): pl.pallas_call(functools.partial(kernel, groups=groups, owners=owners), o...  109 us

profile of v3, /device:TPU:1, one launch (start us, length us, event | category | flops | bytes accessed | tf_op | source)
XLA Modules:
  0.0 111.0 jit_solution(429650803867375052)
XLA Ops:
  0.6 109.0 %shard_map.49 = f32[3,4,128]{2,1,0:T(4,128)} custom-call(f32[512,768]{1,0:T(8,128)} %emb_hbm.1, s32[4,128]{1,0:T(4,128)} %bitcast.7), custom_call_target="tpu_custom_call" | custom-call | tf_op jit(solution)/shard_map/pallas_call | solution.py:306
  109.7 1.3 %slice_bitcast_fusion = (f32[512]{0:T(512)}, f32[512]{0:T(512)}, f32[512]{0:T(512)}) fusion(f32[3,4,128]{2,1,0:T(4,128)} %shard_map.49), kind=kLoop, calls=%fused_computation | loop fusion | bytes 12288 | tf_op jit(solution)/shard_map/reshape;squeeze | solution.py:334

commit v4 on v3

--- a/solution.py
+++ b/solution.py
@@ -12,6 +12,10 @@
 STAGE = 8
 PIECE = 1
 PACK = 4
+BASE = 16
+POOL = 64
+FULL = 1000.0
+LEAD = 8
 MESH = pl.DeviceIdType.MESH
 
 
@@ -21,7 +25,7 @@
     return jnp.where(j % 2 == 1, size, -size)
 
 
-def kernel(
+def padded(
     emb_hbm,
     owner_hbm,
     out_ref,
@@ -296,15 +300,488 @@
             out_ref[which, a : a + 1, :] = line[:, a * 128 : (a + 1) * 128]
 
 
-def local(embeddings, owner):
+def pooled(
+    emb_hbm,
+    owner_hbm,
+    out_ref,
+    flag_ref,
+    emb,
+    owner_ref,
+    unit,
+    outgoing,
+    side,
+    own,
+    before,
+    after,
+    acc,
+    ret,
+    got,
+    pool_out,
+    pool,
+    key_out,
+    keys,
+    full,
+    load_sem,
+    send_sem,
+    recv_sem,
+    pair_send,
+    pair_recv,
+    ret_send,
+    ret_recv,
+    hop_send,
+    hop_recv,
+    share_send,
+    share_recv,
+    key_hop_send,
+    key_hop_recv,
+    key_share_send,
+    key_share_recv,
+    full_send,
+    full_recv,
+    side_send,
+    side_recv,
+    *,
+    groups,
+    owners,
+):
+    rows, width = emb.shape
+    nz = owners // 2
+    group = lax.axis_index("group")
+    me = lax.axis_index("dev")
+    mez, mec = me // 2, me % 2
+    sibling = 2 * mez + 1 - mec
+    steps = nz // 2
+    per_block = STAGE * CAP // BASE
+    blocks = 2 * owners // per_block
+
+    load_owner = pltpu.make_async_copy(owner_hbm, owner_ref, load_sem.at[0])
+    load_owner.start()
+    load = pltpu.make_async_copy(emb_hbm, emb, load_sem.at[1])
+    load.start()
+
+    def target(k):
+        return 2 * ((mez + ring_offset(k, nz) + nz) % nz) + (mec + k) % 2
+
+    def source(k):
+        return 2 * ((mez - ring_offset(k, nz) + nz) % nz) + (mec + k) % 2
+
+    barrier = pltpu.get_barrier_semaphore()
+
+    def greet(d, carry):
+        pl.semaphore_signal(barrier, inc=1, device_id={"dev": (me + d) % owners}, device_id_type=MESH)
+        return carry
+
+    def greet_group(d, carry):
+        pl.semaphore_signal(barrier, inc=1, device_id={"group": (group + d) % groups}, device_id_type=MESH)
+        return carry
+
+    lax.fori_loop(1, owners, greet, 0)
+    lax.fori_loop(1, groups, greet_group, 0)
+
+    load_owner.wait()
+    owner = jnp.concatenate([owner_ref[a : a + 1, :] for a in range(rows // 128)], axis=1)
+    chunk = lax.broadcasted_iota(jnp.int32, (owners, 1), 0)
+    cluster = 2 * ((mez + ring_offset(chunk, nz) + nz) % nz) + (mec + chunk) % 2
+    hot_f = jnp.where(owner == cluster, 1.0, 0.0)
+    hot_b = hot_f.astype(jnp.bfloat16)
+    earlier_row = lax.broadcasted_iota(jnp.int32, (rows, rows), 0) < lax.broadcasted_iota(
+        jnp.int32, (rows, rows), 1
+    )
+    ahead = jnp.dot(
+        hot_b, jnp.where(earlier_row, 1.0, 0.0).astype(jnp.bfloat16), preferred_element_type=jnp.float32
+    )
+
+    def of_row(per_chunk):
+        return jnp.sum(hot_f * per_chunk, axis=0, keepdims=True).astype(jnp.int32)
+
+    rank = of_row(ahead)
+    chunk_of = of_row(chunk.astype(jnp.float32))
+    count = jnp.sum(hot_f, axis=1, keepdims=True)
+    counts = lax.dot_general(
+        jnp.ones((8, rows), jnp.bfloat16), hot_b, (((1,), (1,)), ((), ())), preferred_element_type=jnp.float32
+    )[0:1, :]
+
+    lane = lax.broadcasted_iota(jnp.int32, (1, owners), 1)
+    spill = jnp.where(lane >= 2, jnp.maximum(counts - BASE, 0.0), 0.0)
+
+    def way_of(k):
+        return 1 - (k // 2) % 2
+
+    same_way = way_of(lane) == way_of(chunk)
+    start = jnp.sum(jnp.where(same_way & (lane < chunk), spill, 0.0), axis=1, keepdims=True)
+    most = jnp.max(jnp.sum(jnp.where(same_way, spill, 0.0), axis=1, keepdims=True), axis=0, keepdims=True)
+    at = of_row(start) + rank - BASE
+    spilled = (rank >= BASE) & (chunk_of >= 2) & (at < POOL)
+    pool_slot = jnp.where(spilled, way_of(chunk_of) * POOL + at, -1)
+    hops = (chunk_of // 2 + 1) // 2
+    key = jnp.where(spilled, ((hops - 1) * 2 + chunk_of % 2) * BASE + rank - BASE + 1, 0)
+    base_slot = jnp.where(rank < BASE, chunk_of * BASE + rank, -1)
+    side_slot = jnp.where((rank >= BASE) & (chunk_of < 2), chunk_of * BASE + rank - BASE, -1)
+
+    def pick(slot_of, count_, start_=0):
+        slot = lax.broadcasted_iota(jnp.int32, (count_, 1), 0) + start_
+        return jnp.where(slot_of == slot, 1.0, 0.0).astype(jnp.bfloat16)
+
+    pooled_rows = pick(pool_slot, 2 * POOL)
+    key_row = lax.dot_general(
+        jnp.broadcast_to(key.astype(jnp.float32), (8, rows)).astype(jnp.bfloat16),
+        pooled_rows,
+        (((1,), (1,)), ((), ())),
+        preferred_element_type=jnp.float32,
+    )[0:1, :]
+    key_out[...] = jnp.where(most > POOL, FULL, key_row)
+
+    load.wait()
+    raw = emb[...]
+    norm = jnp.sum(raw * raw, axis=-1, keepdims=True)
+    unit[...] = (raw * lax.rsqrt(norm + 1e-06)).astype(jnp.bfloat16)
+
+    def packed(chosen):
+        return jnp.dot(chosen, unit[...], preferred_element_type=jnp.float32)
+
+    pool_out[...] = packed(pooled_rows).astype(jnp.bfloat16).reshape(2, POOL, width)
+
+    def remote(src, dst, send, recv, where):
+        return pltpu.make_async_remote_copy(
+            src_ref=src, dst_ref=dst, send_sem=send, recv_sem=recv, device_id=where, device_id_type=MESH
+        )
+
+    def beyond(way):
+        return {"dev": 2 * ((mez + (1, nz - 1)[way]) % nz) + mec}
+
+    def hop(s, way):
+        return remote(
+            pool_out.at[way] if s == 0 else pool.at[s, way, 0],
+            pool.at[s + 1, way, 0],
+            hop_send.at[s, way],
+            hop_recv.at[s + 1, way],
+            beyond(way),
+        )
+
+    def key_hop(s, way):
+        return remote(
+            key_out if s == 0 else keys.at[s, way, 0],
+            keys.at[s + 1, way, 0],
+            key_hop_send.at[s, way],
+            key_hop_recv.at[s + 1, way],
+            beyond(way),
+        )
+
+    def share(s, way):
+        return remote(
+            pool.at[s, way, 0], pool.at[s, way, 1], share_send.at[s, way], share_recv.at[s, way], {"dev": sibling}
+        )
+
+    def key_share(s, way):
+        return remote(
+            key_out if s == 0 else keys.at[s, way, 0],
+            keys.at[s, way, 1],
+            key_share_send.at[s, way],
+            key_share_recv.at[s, way],
+            {"dev": sibling},
+        )
+
+    def ways(s):
+        return (0, 1) if s < steps else (0,)
+
+    def dispatch(k):
+        return remote(
+            outgoing.at[k], own.at[owners + k], send_sem.at[k], recv_sem.at[k], {"dev": target(k)}
+        )
+
+    def start_dispatch(k, carry):
+        dispatch(k).start()
+        return carry
+
+    def to_side():
+        return remote(side, own.at[1], side_send, side_recv, {"dev": sibling})
+
+    def forward(first_, size, sem, way):
+        part = pl.ds(first_, size)
+        return remote(
+            own.at[part],
+            (before if way == 0 else after).at[part],
+            pair_send.at[way, sem],
+            pair_recv.at[way, sem],
+            {"group": (group + (1 if way == 0 else groups - 1)) % groups},
+        )
+
+    def tail_piece(s):
+        if s == 0:
+            return (0, 2, 0)
+        return (4 * s - 2, 4 if s < steps else 2, s)
+
+    def base_piece(p):
+        return (owners + 2 * p, 2, steps + 1 + p)
+
+    pl.semaphore_wait(barrier, owners + groups - 2)
+    for way in (0, 1):
+        key_hop(0, way).start()
+        hop(0, way).start()
+    key_share(0, 0).start()
+
+    in_piece = lax.broadcasted_iota(jnp.int32, (BASE, width), 0).astype(jnp.float32)
+    first = lax.broadcasted_iota(jnp.int32, (BASE, width), 1) == 0
+
+    def with_mark(values, k, offset):
+        empty = first & (in_piece + offset >= count[k : k + 1, :])
+        return jnp.where(empty, DEAD, values).astype(jnp.bfloat16)
+
+    group_of = 8
+    for t in range(owners // group_of):
+        values = packed(pick(base_slot, group_of * BASE, t * group_of * BASE))
+        for c in range(group_of):
+            k = t * group_of + c
+            piece = with_mark(values[c * BASE : (c + 1) * BASE, :], k, 0.0)
+            if k == 0:
+                own[owners] = piece
+            else:
+                outgoing[k] = piece
+        if t == 0:
+            lax.fori_loop(1, LEAD, start_dispatch, 0)
+    values = packed(pick(side_slot, 2 * BASE))
+    own[0] = with_mark(values[:BASE, :], 0, float(BASE))
+    side[...] = with_mark(values[BASE:, :], 1, float(BASE))
+    to_side().start()
+    acc[...] = jnp.full_like(acc, -4.0)
+
+    def forward_both(piece):
+        forward(*piece, 0).start()
+        forward(*piece, 1).start()
+
+    def base_arrives(p, carry):
+        def one(k, inner):
+            dispatch(k).wait_recv()
+            return inner
+
+        lax.fori_loop(2 * p, 2 * p + 2, one, 0)
+        forward_both(base_piece(p))
+        return carry
+
+    def block(which, found, jb, ib, diagonal=False):
+        right = found[pl.ds(jb * per_block, per_block)].reshape(per_block * BASE, width)
+        left = own[pl.ds(ib * per_block, per_block)].reshape(per_block * BASE, width)
+        scores = lax.dot_general(right, left, (((1,), (1,)), ((), ())), preferred_element_type=jnp.float32)
+        drop = right[:, :128].astype(jnp.float32)[:, 0:1] > 1.5
+        size = per_block * BASE
+        if diagonal:
+            drop = drop | (
+                (jb == ib)
+                & (
+                    lax.broadcasted_iota(jnp.int32, (size, size), 0)
+                    == lax.broadcasted_iota(jnp.int32, (size, size), 1)
+                )
+            )
+        scores = jnp.where(drop, -1.0, scores)
+        best = jnp.max(scores.reshape(size // 8, 8, size), axis=0)
+        acc[which, ib] = jnp.maximum(acc[which, ib], best)
+
+    def run(combos, kind, stride_j, start_j, stride_i, start_i):
+        across = 2 if stride_i == 2 else blocks
+
+        def body(x, carry):
+            jb = stride_j * (x // across) + start_j
+            ib = stride_i * (x % across) + start_i
+            if kind == "own":
+                block(0, own, jb, ib, diagonal=True)
+            else:
+                block(1, after, jb, ib)
+                block(2, before, jb, ib)
+            return carry
+
+        lax.fori_loop(0, combos, body, 0)
+
+    wide = lax.broadcasted_iota(jnp.int32, (1, 4 * POOL), 1)
+    tall = lax.broadcasted_iota(jnp.int32, (4 * BASE, 1), 0)
+    narrow = lax.broadcasted_iota(jnp.int32, (1, 128), 1)
+
+    def select(s):
+        parts = []
+        for way in ways(s):
+            zero, one = keys[s, way, 0], keys[s, way, 1]
+            if way == 0:
+                parts.append(jnp.where(narrow < POOL, zero, pltpu.roll(one, POOL, 1)))
+            else:
+                parts.append(jnp.where(narrow < POOL, pltpu.roll(zero, POOL, 1), one))
+        n = len(parts)
+        held = jnp.concatenate(parts, axis=1)
+        lanes, outs = wide[:, : 2 * n * POOL], tall[: 2 * n * BASE, :]
+        wanted = (((s - 1) * 2 + (outs // BASE) % 2) * BASE + outs % BASE + 1).astype(jnp.float32)
+        match = (lanes // POOL == outs // BASE) & (held == wanted)
+        chosen = jnp.where(match, 1.0, 0.0)
+        there = pool[s, 0:n].reshape(2 * n * POOL, width)
+        values_ = jnp.dot(chosen.astype(jnp.bfloat16), there, preferred_element_type=jnp.float32)
+        none = jnp.sum(chosen, axis=1, keepdims=True) < 0.5
+        front = lax.broadcasted_iota(jnp.int32, values_.shape, 1) == 0
+        values_ = jnp.where(front & none, DEAD, values_).astype(jnp.bfloat16)
+        begin, size, _ = tail_piece(s)
+        own[begin : begin + size] = values_.reshape(size, BASE, width)
+
+    to_side().wait_recv()
+    forward_both(tail_piece(0))
+    for s in range(1, steps + 1):
+        for way in ways(s):
+            hop(s - 1, way).wait_recv()
+            key_hop(s - 1, way).wait_recv()
+            if s < steps - way:
+                key_hop(s, way).start()
+                hop(s, way).start()
+            key_share(s, way).start()
+            share(s, way).start()
+        if s < steps:
+            per_step = (owners - LEAD + steps - 2) // (steps - 1)
+            low = min(LEAD + per_step * (s - 1), owners)
+            lax.fori_loop(low, min(low + per_step, owners), start_dispatch, 0)
+        if s == 2:
+            dispatch(1).wait_recv()
+            forward_both(base_piece(0))
+        if s > 2:
+            lax.fori_loop(2 * s - 5, 2 * s - 3, base_arrives, 0)
+        for way in ways(s):
+            share(s, way).wait_recv()
+            key_share(s, way).wait_recv()
+        select(s)
+        forward_both(tail_piece(s))
+        if s == steps - 2:
+            run(4, "own", 2, 0, 2, 0)
+    key_share(0, 0).wait_recv()
+
+    worst = jnp.maximum(key_out[...], keys[0, 0, 1])
+    for s in range(1, steps + 1):
+        for way in ways(s):
+            worst = jnp.maximum(worst, jnp.maximum(keys[s, way, 0], keys[s, way, 1]))
+    full[0] = worst
+
+    def tell(d):
+        return remote(
+            full.at[0], full.at[d], full_send.at[d], full_recv.at[d], {"group": (group + d) % groups}
+        )
+
+    def start_tell(d, carry):
+        tell(d).start()
+        return carry
+
+    lax.fori_loop(1, groups, start_tell, 0)
+
+    def pair_arrives(pieces):
+        for piece in pieces:
+            forward(*piece, 0).wait_recv()
+            forward(*piece, 1).wait_recv()
+
+    def base_pair_arrives(p, carry):
+        pair_arrives([base_piece(p)])
+        return carry
+
+    half = steps // 2
+    done = 2 * steps - 3
+    lax.fori_loop(done, done + 1, base_arrives, 0)
+    pair_arrives([tail_piece(s) for s in range(half + 1)])
+    lax.fori_loop(0, half * 2, base_pair_arrives, 0)
+    run(4, "pair", 2, 0, 2, 0)
+    lax.fori_loop(done + 1, owners // 2, base_arrives, 0)
+    run(8, "own", 2, 1, 1, 0)
+    run(4, "own", 2, 0, 2, 1)
+    run(4, "pair", 2, 0, 2, 1)
+    pair_arrives([tail_piece(s) for s in range(half + 1, steps + 1)])
+    lax.fori_loop(half * 2, owners // 2, base_pair_arrives, 0)
+    run(8, "pair", 2, 1, 1, 0)
+
+    tiles = []
+    for which in range(3):
+        parts = []
+        for b in range(blocks):
+            best = jnp.max(acc[which, b], axis=0, keepdims=True)
+            parts += [best[:, h * 128 : (h + 1) * 128] for h in range(per_block * BASE // 128)]
+        early = jnp.concatenate(parts[len(parts) // 2 :], axis=0)
+        late = jnp.concatenate(parts[: len(parts) // 2], axis=0)
+        tiles += [early, late]
+    spot = lax.broadcasted_iota(jnp.int32, tiles[0].shape, 1) // BASE
+    per_tile = 128 // BASE
+    for j in range(per_tile):
+        mixed = tiles[0] if j == 0 else pltpu.roll(tiles[0], (-BASE * j) % 128, 1)
+        for u in range(1, 6):
+            moved = tiles[u] if u == j else pltpu.roll(tiles[u], (BASE * (u - j)) % 128, 1)
+            mixed = jnp.where(spot >= u, moved, mixed)
+        for t in range(owners // per_tile):
+            k = per_tile * t + j
+            if k == 0:
+                got[k] = mixed[t : t + 1, :]
+            else:
+                ret[k] = mixed[t : t + 1, :]
+
+    def give_back(k):
+        return remote(ret.at[k], got.at[k], ret_send.at[k], ret_recv.at[k], {"dev": source(k)})
+
+    def start_back(k, carry):
+        give_back(k).start()
+        return carry
+
+    lax.fori_loop(1, owners, start_back, 0)
+
+    def drain(k, carry):
+        dispatch(k).wait_send()
+        return carry
+
+    lax.fori_loop(1, owners, drain, 0)
+    to_side().wait_send()
+    key_share(0, 0).wait_send()
+    for s in range(steps + 1):
+        for way in (0, 1):
+            if s < steps - way:
+                hop(s, way).wait_send()
+                key_hop(s, way).wait_send()
+        if s > 0:
+            for way in ways(s):
+                share(s, way).wait_send()
+                key_share(s, way).wait_send()
+        forward(*tail_piece(s), 0).wait_send()
+        forward(*tail_piece(s), 1).wait_send()
+
+    def drain_pair(p, carry):
+        forward(*base_piece(p), 0).wait_send()
+        forward(*base_piece(p), 1).wait_send()
+        return carry
+
+    lax.fori_loop(0, owners // 2, drain_pair, 0)
+
+    def wait_tell(d, carry):
+        tell(d).wait()
+        return carry
+
+    lax.fori_loop(1, groups, wait_tell, 0)
+    flag_ref[...] = jnp.max(full[...], axis=0)
+
+    def wait_back(k, carry):
+        give_back(k).wait()
+        return carry
+
+    lax.fori_loop(1, owners, wait_back, 0)
+
+    table = got[...].reshape(owners, 128)
+    high = table.astype(jnp.bfloat16)
+    rest = table - high.astype(jnp.float32)
+    middle = rest.astype(jnp.bfloat16)
+    low_part = (rest - middle.astype(jnp.float32)).astype(jnp.bfloat16)
+    stacked = jnp.concatenate([high, middle, low_part], axis=0)
+    picks = jnp.concatenate([hot_b, hot_b, hot_b], axis=0)
+    found = lax.dot_general(stacked, picks, (((0,), (0,)), ((), ())), preferred_element_type=jnp.float32)
+    mine = lax.broadcasted_iota(jnp.int32, (CAP, 1), 0) == rank
+    for which in range(3):
+        kept = jnp.where(mine, found[which * CAP : (which + 1) * CAP, :], 0.0)
+        line = jnp.sum(kept, axis=0, keepdims=True)
+        for a in range(rows // 128):
+            out_ref[which, a : a + 1, :] = line[:, a * 128 : (a + 1) * 128]
+
+
+def all_slots(embeddings, owner):
     owners = lax.axis_size("dev")
     groups = lax.axis_size("group")
     rows, width = embeddings.shape
     vmem = pl.BlockSpec(memory_space=pltpu.VMEM)
     slots = (owners, CAP, width)
     hbm = pl.BlockSpec(memory_space=pltpu.HBM)
-    out = pl.pallas_call(
-        functools.partial(kernel, groups=groups, owners=owners),
+    return pl.pallas_call(
+        functools.partial(padded, groups=groups, owners=owners),
         out_shape=jax.ShapeDtypeStruct((3, rows // 128, 128), jnp.float32),
         in_specs=[hbm, hbm],
         out_specs=vmem,
@@ -328,9 +805,78 @@
             pltpu.SemaphoreType.DMA((owners,)),
         ],
         compiler_params=pltpu.CompilerParams(
+            collective_id=1, has_side_effects=True, vmem_limit_bytes=60 * 1024 * 1024
+        ),
+    )(embeddings, owner)
+
+
+def few_slots(embeddings, owner):
+    owners = lax.axis_size("dev")
+    groups = lax.axis_size("group")
+    rows, width = embeddings.shape
+    steps = owners // 4
+    vmem = pl.BlockSpec(memory_space=pltpu.VMEM)
+    hbm = pl.BlockSpec(memory_space=pltpu.HBM)
+    entries = (2 * owners, BASE, width)
+    size = STAGE * CAP
+    pieces = steps + 1 + owners // 2
+    ring = pltpu.SemaphoreType.DMA((steps + 1, 2))
+    return pl.pallas_call(
+        functools.partial(pooled, groups=groups, owners=owners),
+        out_shape=(
+            jax.ShapeDtypeStruct((3, rows // 128, 128), jnp.float32),
+            jax.ShapeDtypeStruct((1, 128), jnp.float32),
+        ),
+        in_specs=[hbm, hbm],
+        out_specs=(vmem, vmem),
+        scratch_shapes=[
+            pltpu.VMEM((rows, width), jnp.float32),
+            pltpu.VMEM((rows // 128, 128), jnp.int32),
+            pltpu.VMEM((rows, width), jnp.bfloat16),
+            pltpu.VMEM((owners, BASE, width), jnp.bfloat16),
+            pltpu.VMEM((BASE, width), jnp.bfloat16),
+            pltpu.VMEM(entries, jnp.bfloat16),
+            pltpu.VMEM(entries, jnp.bfloat16),
+            pltpu.VMEM(entries, jnp.bfloat16),
+            pltpu.VMEM((3, 2 * owners * BASE // size, 8, size), jnp.float32),
+            pltpu.VMEM((owners, 1, 128), jnp.float32),
+            pltpu.VMEM((owners, 1, 128), jnp.float32),
+            pltpu.VMEM((2, POOL, width), jnp.bfloat16),
+            pltpu.VMEM((steps + 1, 2, 2, POOL, width), jnp.bfloat16),
+            pltpu.VMEM((1, 128), jnp.float32),
+            pltpu.VMEM((steps + 1, 2, 2, 1, 128), jnp.float32),
+            pltpu.VMEM((groups, 1, 128), jnp.float32),
+            pltpu.SemaphoreType.DMA((2,)),
+            pltpu.SemaphoreType.DMA((owners,)),
+            pltpu.SemaphoreType.DMA((owners,)),
+            pltpu.SemaphoreType.DMA((2, pieces)),
+            pltpu.SemaphoreType.DMA((2, pieces)),
+            pltpu.SemaphoreType.DMA((owners,)),
+            pltpu.SemaphoreType.DMA((owners,)),
+            ring,
+            ring,
+            ring,
+            ring,
+            ring,
+            ring,
+            ring,
+            ring,
+            pltpu.SemaphoreType.DMA((groups,)),
+            pltpu.SemaphoreType.DMA((groups,)),
+            pltpu.SemaphoreType.DMA,
+            pltpu.SemaphoreType.DMA,
+        ],
+        compiler_params=pltpu.CompilerParams(
             collective_id=0, has_side_effects=True, vmem_limit_bytes=60 * 1024 * 1024
         ),
-    )(embeddings, owner.reshape(rows // 128, 128))
+    )(embeddings, owner)
+
+
+def local(embeddings, owner):
+    rows = embeddings.shape[0]
+    lines = owner.reshape(rows // 128, 128)
+    out, flag = few_slots(embeddings, lines)
+    out = lax.cond(jnp.max(flag) > FULL / 2, lambda e, o, kept: all_slots(e, o), lambda e, o, kept: kept, embeddings, lines, out)
     return tuple(out[which].reshape(rows) for which in range(3))
 
 

time: 111 us -> 101 us (0.910)
  Pallas kernels: 109 us -> 97 us
  other arithmetic: 0 us -> 1.24 us
    pallas_call x1, Pallas kernels: 109 us -> 97 us  [few_slots(): pl.pallas_call(functools.partial(pooled, groups=groups, owners=owners), o...]
    reduce_max x0 -> x1, other arithmetic: none -> 1.24 us  [local(): jnp.max(flag) > FULL / 2]
where the time goes in v4:
time: 101 us; the launch traced here: 100 us
  Pallas kernels  97 us (96%)
  between operations  1.33 us (1%)
  other arithmetic  1.24 us (1%)
    pallas_call x1, Pallas kernels, few_slots(): pl.pallas_call(functools.partial(pooled, groups=groups, owners=owners), o...  97 us

profile of v4, /device:TPU:1, one launch (start us, length us, event | category | flops | bytes accessed | tf_op | source)
XLA Modules:
  0.0 100.4 jit_solution(18132919452136953883)
XLA Ops:
  0.6 0.0 copy-start
  0.6 0.0 copy-start.1
  0.6 97.0 %shard_map.49 = (f32[3,4,128]{2,1,0:T(4,128)S(1)}, f32[1,128]{1,0:T(1,128)}) custom-call(f32[512,768]{1,0:T(8,128)} %emb_hbm.1, s32[4,128]{1,0:T(4,128)} %bitcast.7), custom_call_target="tpu_custom_call" | custom-call | tf_op jit(solution)/shard_map/pallas_call | solution.py:824
  97.7 1.2 %reduce_max.9 = f32[]{:T(128)} reduce(f32[1,128]{1,0:T(1,128)} %get-tuple-element.15, f32[]{:T(128)} %constant.0.clone.1), dimensions={0,1}, to_apply=%region_0.0 | reduce | flops 127 | bytes 520 | tf_op jit(solution)/shard_map/reduce_max | solution.py:879
  99.6 0.0 copy-done
  99.6 0.0 copy-done.1
  99.6 0.2 conditional.1
  99.8 0.6 slice_bitcast_fusion
Async XLA Ops:
  0.6 99.0 %copy-start = (f32[512,768]{1,0:T(8,128)S(1)}, f32[512,768]{1,0:T(8,128)}, u32[]{:S(2)}) copy-start(f32[512,768]{1,0:T(8,128)} %emb_hbm.1) | copy-start | bytes 4718596
  0.6 99.0 %copy-start.1 = (s32[512]{0:T(512)S(1)}, s32[512]{0:T(512)}, u32[]{:S(2)}) copy-start(s32[512]{0:T(512)} %param.5) | copy-start | bytes 6148

commit v5 on v4

--- a/solution.py
+++ b/solution.py
@@ -17,6 +17,10 @@
 FULL = 1000.0
 LEAD = 8
 MESH = pl.DeviceIdType.MESH
+
+
+def room(step):
+    return 64 if step <= 3 else 48 if step <= 6 else 32
 
 
 def ring_offset(k, nz):
@@ -408,8 +412,13 @@
         return 1 - (k // 2) % 2
 
     same_way = way_of(lane) == way_of(chunk)
-    start = jnp.sum(jnp.where(same_way & (lane < chunk), spill, 0.0), axis=1, keepdims=True)
-    most = jnp.max(jnp.sum(jnp.where(same_way, spill, 0.0), axis=1, keepdims=True), axis=0, keepdims=True)
+    start = jnp.sum(jnp.where(same_way & (lane > chunk), spill, 0.0), axis=1, keepdims=True)
+    filled = jnp.sum(jnp.where(same_way & (lane >= chunk), spill, 0.0), axis=1, keepdims=True)
+    step_of = (chunk // 2 + 1) // 2
+    space = jnp.full((owners, 1), float(room(1)), jnp.float32)
+    for s in range(2, steps + 1):
+        space = jnp.where(step_of >= s, float(room(s)), space)
+    excess = jnp.max(jnp.where(chunk >= 2, filled - space, -1.0), axis=0, keepdims=True)
     at = of_row(start) + rank - BASE
     spilled = (rank >= BASE) & (chunk_of >= 2) & (at < POOL)
     pool_slot = jnp.where(spilled, way_of(chunk_of) * POOL + at, -1)
@@ -429,7 +438,7 @@
         (((1,), (1,)), ((), ())),
         preferred_element_type=jnp.float32,
     )[0:1, :]
-    key_out[...] = jnp.where(most > POOL, FULL, key_row)
+    key_out[...] = jnp.where(excess > 0.0, FULL, key_row)
 
     load.wait()
     raw = emb[...]
@@ -450,9 +459,10 @@
         return {"dev": 2 * ((mez + (1, nz - 1)[way]) % nz) + mec}
 
     def hop(s, way):
+        part = pl.ds(0, room(s + 1))
         return remote(
-            pool_out.at[way] if s == 0 else pool.at[s, way, 0],
-            pool.at[s + 1, way, 0],
+            pool_out.at[way, part] if s == 0 else pool.at[s, way, 0, part],
+            pool.at[s + 1, way, 0, part],
             hop_send.at[s, way],
             hop_recv.at[s + 1, way],
             beyond(way),
@@ -468,8 +478,13 @@
         )
 
     def share(s, way):
+        part = pl.ds(0, room(s))
         return remote(
-            pool.at[s, way, 0], pool.at[s, way, 1], share_send.at[s, way], share_recv.at[s, way], {"dev": sibling}
+            pool.at[s, way, 0, part],
+            pool.at[s, way, 1, part],
+            share_send.at[s, way],
+            share_recv.at[s, way],
+            {"dev": sibling},
         )
 
     def key_share(s, way):
@@ -544,6 +559,11 @@
     side[...] = with_mark(values[BASE:, :], 1, float(BASE))
     to_side().start()
     acc[...] = jnp.full_like(acc, -4.0)
+    for s in range(1, steps + 1):
+        if room(s) < POOL:
+            for way in ways(s):
+                for core in (0, 1):
+                    pool[s, way, core, room(s) :] = jnp.zeros((POOL - room(s), width), jnp.bfloat16)
 
     def forward_both(piece):
         forward(*piece, 0).start()
@@ -632,16 +652,16 @@
             per_step = (owners - LEAD + steps - 2) // (steps - 1)
             low = min(LEAD + per_step * (s - 1), owners)
             lax.fori_loop(low, min(low + per_step, owners), start_dispatch, 0)
+        for way in ways(s):
+            share(s, way).wait_recv()
+            key_share(s, way).wait_recv()
+        select(s)
+        forward_both(tail_piece(s))
         if s == 2:
             dispatch(1).wait_recv()
             forward_both(base_piece(0))
         if s > 2:
             lax.fori_loop(2 * s - 5, 2 * s - 3, base_arrives, 0)
-        for way in ways(s):
-            share(s, way).wait_recv()
-            key_share(s, way).wait_recv()
-        select(s)
-        forward_both(tail_piece(s))
         if s == steps - 2:
             run(4, "own", 2, 0, 2, 0)
     key_share(0, 0).wait_recv()
@@ -683,8 +703,9 @@
     run(4, "own", 2, 0, 2, 1)
     run(4, "pair", 2, 0, 2, 1)
     pair_arrives([tail_piece(s) for s in range(half + 1, steps + 1)])
+    run(4, "pair", 0, 1, 1, 0)
     lax.fori_loop(half * 2, owners // 2, base_pair_arrives, 0)
-    run(8, "pair", 2, 1, 1, 0)
+    run(4, "pair", 0, 3, 1, 0)
 
     tiles = []
     for which in range(3):
@@ -713,7 +734,7 @@
         return remote(ret.at[k], got.at[k], ret_send.at[k], ret_recv.at[k], {"dev": source(k)})
 
     def start_back(k, carry):
-        give_back(k).start()
+        give_back(owners - k).start()
         return carry
 
     lax.fori_loop(1, owners, start_back, 0)
@@ -749,7 +770,7 @@
         return carry
 
     lax.fori_loop(1, groups, wait_tell, 0)
-    flag_ref[...] = jnp.max(full[...], axis=0)
+    flag_ref[0, 0] = jnp.max(full[...])
 
     def wait_back(k, carry):
         give_back(k).wait()
@@ -825,10 +846,10 @@
         functools.partial(pooled, groups=groups, owners=owners),
         out_shape=(
             jax.ShapeDtypeStruct((3, rows // 128, 128), jnp.float32),
-            jax.ShapeDtypeStruct((1, 128), jnp.float32),
+            jax.ShapeDtypeStruct((1, 1), jnp.float32),
         ),
         in_specs=[hbm, hbm],
-        out_specs=(vmem, vmem),
+        out_specs=(vmem, pl.BlockSpec(memory_space=pltpu.SMEM)),
         scratch_shapes=[
             pltpu.VMEM((rows, width), jnp.float32),
             pltpu.VMEM((rows // 128, 128), jnp.int32),
@@ -876,7 +897,7 @@
     rows = embeddings.shape[0]
     lines = owner.reshape(rows // 128, 128)
     out, flag = few_slots(embeddings, lines)
-    out = lax.cond(jnp.max(flag) > FULL / 2, lambda e, o, kept: all_slots(e, o), lambda e, o, kept: kept, embeddings, lines, out)
+    out = lax.cond(flag[0, 0] > FULL / 2, lambda e, o, kept: all_slots(e, o), lambda e, o, kept: kept, embeddings, lines, out)
     return tuple(out[which].reshape(rows) for which in range(3))
 
 

time: 101 us -> 96.6 us (0.956)
  Pallas kernels: 97 us -> 94.4 us
  other arithmetic: 1.24 us -> 0 us
    pallas_call x1, Pallas kernels: 97 us -> 94.4 us  [few_slots(): pl.pallas_call(functools.partial(pooled, groups=groups, owners=owners), o...]
    reduce_max x1 -> x0, other arithmetic: 1.24 us -> none  [local(): jnp.max(flag) > FULL / 2]
where the time goes in v5:
time: 96.6 us; the launch traced here: 96.4 us
  Pallas kernels  94.4 us (98%)
  between operations  1.24 us (1%)
    pallas_call x1, Pallas kernels, few_slots(): pl.pallas_call(functools.partial(pooled, groups=groups, owners=owners), o...  94.4 us

profile of v5, /device:TPU:1, one launch (start us, length us, event | category | flops | bytes accessed | tf_op | source)
XLA Modules:
  0.0 96.4 jit_solution(6569742356124598807)
XLA Ops:
  0.6 0.0 copy-start
  0.6 0.0 copy-start.1
  0.6 94.4 %shard_map.49 = (f32[3,4,128]{2,1,0:T(4,128)S(1)}, f32[1,1]{1,0:T(1,128)}) custom-call(f32[512,768]{1,0:T(8,128)} %emb_hbm.1, s32[4,128]{1,0:T(4,128)} %bitcast.8), custom_call_target="tpu_custom_call" | custom-call | tf_op jit(solution)/shard_map/pallas_call | solution.py:845
  95.6 0.0 copy-done
  95.6 0.0 copy-done.1
  95.7 0.2 conditional.1
  95.8 0.6 slice_bitcast_fusion
Async XLA Ops:
  0.6 95.0 %copy-start = (f32[512,768]{1,0:T(8,128)S(1)}, f32[512,768]{1,0:T(8,128)}, u32[]{:S(2)}) copy-start(f32[512,768]{1,0:T(8,128)} %emb_hbm.1) | copy-start | bytes 4718596
  0.6 95.0 %copy-start.1 = (s32[512]{0:T(512)S(1)}, s32[512]{0:T(512)}, u32[]{:S(2)}) copy-start(s32[512]{0:T(512)} %param.5) | copy-start | bytes 6148

commit v6 on v5

--- a/solution.py
+++ b/solution.py
@@ -15,6 +15,7 @@
 BASE = 16
 POOL = 64
 FULL = 1000.0
+ORDER = (0, 3, 1, 2)
 LEAD = 8
 MESH = pl.DeviceIdType.MESH
 
@@ -357,6 +358,7 @@
     steps = nz // 2
     per_block = STAGE * CAP // BASE
     blocks = 2 * owners // per_block
+    group_of = owners // len(ORDER)
 
     load_owner = pltpu.make_async_copy(owner_hbm, owner_ref, load_sem.at[0])
     load_owner.start()
@@ -458,13 +460,14 @@
     def beyond(way):
         return {"dev": 2 * ((mez + (1, nz - 1)[way]) % nz) + mec}
 
-    def hop(s, way):
-        part = pl.ds(0, room(s + 1))
+    def hop(s, way, half_):
+        cut = 32 if room(s + 1) > 32 else 16
+        part = pl.ds(0, cut) if half_ == 0 else pl.ds(cut, room(s + 1) - cut)
         return remote(
             pool_out.at[way, part] if s == 0 else pool.at[s, way, 0, part],
             pool.at[s + 1, way, 0, part],
-            hop_send.at[s, way],
-            hop_recv.at[s + 1, way],
+            hop_send.at[s, way, half_],
+            hop_recv.at[s + 1, way, half_],
             beyond(way),
         )
 
@@ -499,9 +502,17 @@
     def ways(s):
         return (0, 1) if s < steps else (0,)
 
-    def dispatch(k):
+    def dispatch(n):
+        turn = n // group_of
+        part = jnp.int32(ORDER[-1])
+        for other in range(len(ORDER) - 1):
+            part = jnp.where(turn == other, ORDER[other], part)
         return remote(
-            outgoing.at[k], own.at[owners + k], send_sem.at[k], recv_sem.at[k], {"dev": target(k)}
+            outgoing.at[n],
+            own.at[owners + n],
+            send_sem.at[n],
+            recv_sem.at[n],
+            {"dev": target(part * group_of + n % group_of)},
         )
 
     def start_dispatch(k, carry):
@@ -532,7 +543,9 @@
     pl.semaphore_wait(barrier, owners + groups - 2)
     for way in (0, 1):
         key_hop(0, way).start()
-        hop(0, way).start()
+    for half_ in (0, 1):
+        for way in (0, 1):
+            hop(0, way, half_).start()
     key_share(0, 0).start()
 
     in_piece = lax.broadcasted_iota(jnp.int32, (BASE, width), 0).astype(jnp.float32)
@@ -542,16 +555,15 @@
         empty = first & (in_piece + offset >= count[k : k + 1, :])
         return jnp.where(empty, DEAD, values).astype(jnp.bfloat16)
 
-    group_of = 8
     for t in range(owners // group_of):
-        values = packed(pick(base_slot, group_of * BASE, t * group_of * BASE))
+        values = packed(pick(base_slot, group_of * BASE, ORDER[t] * group_of * BASE))
         for c in range(group_of):
-            k = t * group_of + c
-            piece = with_mark(values[c * BASE : (c + 1) * BASE, :], k, 0.0)
-            if k == 0:
+            n = t * group_of + c
+            piece = with_mark(values[c * BASE : (c + 1) * BASE, :], ORDER[t] * group_of + c, 0.0)
+            if n == 0:
                 own[owners] = piece
             else:
-                outgoing[k] = piece
+                outgoing[n] = piece
         if t == 0:
             lax.fori_loop(1, LEAD, start_dispatch, 0)
     values = packed(pick(side_slot, 2 * BASE))
@@ -640,12 +652,15 @@
     to_side().wait_recv()
     forward_both(tail_piece(0))
     for s in range(1, steps + 1):
+        for half_ in (0, 1):
+            for way in ways(s):
+                hop(s - 1, way, half_).wait_recv()
+                if s < steps - way:
+                    hop(s, way, half_).start()
         for way in ways(s):
-            hop(s - 1, way).wait_recv()
             key_hop(s - 1, way).wait_recv()
             if s < steps - way:
                 key_hop(s, way).start()
-                hop(s, way).start()
             key_share(s, way).start()
             share(s, way).start()
         if s < steps:
@@ -713,7 +728,7 @@
         for b in range(blocks):
             best = jnp.max(acc[which, b], axis=0, keepdims=True)
             parts += [best[:, h * 128 : (h + 1) * 128] for h in range(per_block * BASE // 128)]
-        early = jnp.concatenate(parts[len(parts) // 2 :], axis=0)
+        early = jnp.concatenate([parts[len(parts) // 2 + ORDER.index(t)] for t in range(len(ORDER))], axis=0)
         late = jnp.concatenate(parts[: len(parts) // 2], axis=0)
         tiles += [early, late]
     spot = lax.broadcasted_iota(jnp.int32, tiles[0].shape, 1) // BASE
@@ -749,7 +764,8 @@
     for s in range(steps + 1):
         for way in (0, 1):
             if s < steps - way:
-                hop(s, way).wait_send()
+                hop(s, way, 0).wait_send()
+                hop(s, way, 1).wait_send()
                 key_hop(s, way).wait_send()
         if s > 0:
             for way in ways(s):
@@ -842,6 +858,7 @@
     size = STAGE * CAP
     pieces = steps + 1 + owners // 2
     ring = pltpu.SemaphoreType.DMA((steps + 1, 2))
+    halves = pltpu.SemaphoreType.DMA((steps + 1, 2, 2))
     return pl.pallas_call(
         functools.partial(pooled, groups=groups, owners=owners),
         out_shape=(
@@ -874,8 +891,8 @@
             pltpu.SemaphoreType.DMA((2, pieces)),
             pltpu.SemaphoreType.DMA((owners,)),
             pltpu.SemaphoreType.DMA((owners,)),
-            ring,
-            ring,
+            halves,
+            halves,
             ring,
             ring,
             ring,

time: 96.6 us -> 95.1 us (0.984)
  Pallas kernels: 94.4 us -> 92.9 us
    pallas_call x1, Pallas kernels: 94.4 us -> 92.9 us  [few_slots(): pl.pallas_call(functools.partial(pooled, groups=groups, owners=owners), o...]
where the time goes in v6:
time: 95.1 us; the launch traced here: 94.9 us
  Pallas kernels  92.9 us (98%)
  between operations  1.24 us (1%)
    pallas_call x1, Pallas kernels, few_slots(): pl.pallas_call(functools.partial(pooled, groups=groups, owners=owners), o...  92.9 us

profile of v6, /device:TPU:1, one launch (start us, length us, event | category | flops | bytes accessed | tf_op | source)
XLA Modules:
  0.0 94.9 jit_solution(7578535305576643908)
XLA Ops:
  0.6 0.0 copy-start
  0.6 0.0 copy-start.1
  0.6 92.9 %shard_map.49 = (f32[3,4,128]{2,1,0:T(4,128)S(1)}, f32[1,1]{1,0:T(1,128)}) custom-call(f32[512,768]{1,0:T(8,128)} %emb_hbm.1, s32[4,128]{1,0:T(4,128)} %bitcast.8), custom_call_target="tpu_custom_call" | custom-call | tf_op jit(solution)/shard_map/pallas_call | solution.py:862
  94.1 0.0 copy-done
  94.1 0.0 copy-done.1
  94.1 0.2 conditional.1
  94.3 0.6 slice_bitcast_fusion
Async XLA Ops:
  0.6 93.5 %copy-start = (f32[512,768]{1,0:T(8,128)S(1)}, f32[512,768]{1,0:T(8,128)}, u32[]{:S(2)}) copy-start(f32[512,768]{1,0:T(8,128)} %emb_hbm.1) | copy-start | bytes 4718596
  0.6 93.5 %copy-start.1 = (s32[512]{0:T(512)S(1)}, s32[512]{0:T(512)}, u32[]{:S(2)}) copy-start(s32[512]{0:T(512)} %param.5) | copy-start | bytes 6148

commit v7 on v6

--- a/solution.py
+++ b/solution.py
@@ -709,11 +709,10 @@
 
     half = steps // 2
     done = 2 * steps - 3
-    lax.fori_loop(done, done + 1, base_arrives, 0)
+    lax.fori_loop(done, owners // 2, base_arrives, 0)
     pair_arrives([tail_piece(s) for s in range(half + 1)])
     lax.fori_loop(0, half * 2, base_pair_arrives, 0)
     run(4, "pair", 2, 0, 2, 0)
-    lax.fori_loop(done + 1, owners // 2, base_arrives, 0)
     run(8, "own", 2, 1, 1, 0)
     run(4, "own", 2, 0, 2, 1)
     run(4, "pair", 2, 0, 2, 1)

time: 95.1 us -> 95.1 us (level)
  no operation moved by 1% of the time
where the time goes in v7:
time: 95.1 us; the launch traced here: 94.9 us
  Pallas kernels  92.9 us (98%)
  between operations  1.24 us (1%)
    pallas_call x1, Pallas kernels, few_slots(): pl.pallas_call(functools.partial(pooled, groups=groups, owners=owners), o...  92.9 us

profile of v7, /device:TPU:1, one launch (start us, length us, event | category | flops | bytes accessed | tf_op | source)
XLA Modules:
  0.0 94.9 jit_solution(8529881550174562596)
XLA Ops:
  0.6 0.0 copy-start
  0.6 0.0 copy-start.1
  0.6 92.9 %shard_map.49 = (f32[3,4,128]{2,1,0:T(4,128)S(1)}, f32[1,1]{1,0:T(1,128)}) custom-call(f32[512,768]{1,0:T(8,128)} %emb_hbm.1, s32[4,128]{1,0:T(4,128)} %bitcast.8), custom_call_target="tpu_custom_call" | custom-call | tf_op jit(solution)/shard_map/pallas_call | solution.py:861
  94.1 0.0 copy-done
  94.1 0.0 copy-done.1
  94.1 0.2 conditional.1
  94.3 0.6 slice_bitcast_fusion
Async XLA Ops:
  0.6 93.5 %copy-start = (f32[512,768]{1,0:T(8,128)S(1)}, f32[512,768]{1,0:T(8,128)}, u32[]{:S(2)}) copy-start(f32[512,768]{1,0:T(8,128)} %emb_hbm.1) | copy-start | bytes 4718596
  0.6 93.5 %copy-start.1 = (s32[512]{0:T(512)S(1)}, s32[512]{0:T(512)}, u32[]{:S(2)}) copy-start(s32[512]{0:T(512)} %param.5) | copy-start | bytes 6148
